TPU v7x, 32 devices: a whole 2x2x4 slice. The times are simulated.
32 devices in a mesh: dp: 8 (over z, x), owner: 4 (over y, core).
Axes of the slice: x: 2, y: 2, z: 4, core: 2. Of those that a mesh axis runs over, the one named last changes fastest.
Arguments:
- hidden: bfloat16 [8192, 6912], P(('dp', 'owner')), may hold values from -6 to 6
- grad_out: bfloat16 [8192, 2560], P(('dp', 'owner')), may hold values from -6 to 6
- block_list: int32 [128, 2], replicated, may hold values from 0 to 107, as said below
- live_block_count: int32 [32], replicated, may hold values from 1 to 4, as said below
- master: float32 [128, 4096], P(('dp', 'owner')), may hold values from -6 to 6
- moment: float32 [128, 4096], P(('dp', 'owner')), may hold values from -6 to 6
- variance: float32 [128, 4096], P(('dp', 'owner')), may hold values from 0.25 to 4
Outputs:
- new_master: float32 [128, 4096], P(('dp', 'owner'))
- new_moment: float32 [128, 4096], P(('dp', 'owner'))
- new_variance: float32 [128, 4096], P(('dp', 'owner'))
- clipped_grad: float32 [128, 4096], P(('dp', 'owner'))
- published: bfloat16 [128, 4096], replicated
Inputs may be any that keep to these rules, and one draw needn't show every extreme that they name: `block_list`: each row names a block: its row index below 108, its column index below 40; all rows name different blocks. Rows 4 o to 4 o + 3 are owner o's slots; owner o is the device whose index along dp is o // 4 and whose index along the mesh axis `owner` is o mod 4. Owner o's first live_block_count[o] slots are live, the rest padding; some owner's slots are all live.
All inputs are finite; a program needn't handle non-finite values.
Results may differ from a plain program's by a relative error of at most 0.001.
Values may be sent and summed in bfloat16 or wider, within the bound.
No kernel may reach another device: no remote copies, remote signals or barrier semaphores. Data moves between devices by JAX's collectives and lax.ppermute only.
A program may use at most 128 MiB of HBM per device.

v0:
```python
import functools

import jax
import jax.numpy as jnp
from jax import lax
from jax.experimental import pallas as pl
from jax.experimental.pallas import tpu as pltpu
from jax.sharding import Mesh
from jax.sharding import PartitionSpec as P

SIDE = 64
LANES = 128
SLOTS = 4
PAIRS = SLOTS // 2
BLOCK = SIDE * SIDE
TILES = BLOCK // LANES
EXP_ROWS = 8
CODE_BITS = 13
CORES = 2
AXES = ("chip", "core")
INV_LN2 = 1.4426950408889634


def turn_kernel(grad_ref, turned_ref):
    for k in range(grad_ref.shape[1] // LANES):
        turned_ref[pl.ds(k * LANES, LANES), :] = grad_ref[:, pl.ds(k * LANES, LANES)].T


def block_products(core, blocks_ref, hidden_ref, turned_ref, out_ref):
    low_lane = lax.broadcasted_iota(jnp.int32, (SIDE, LANES), 1) < SIDE

    def one_chip(chip, carry):
        owner = chip * CORES + core
        for pair in range(PAIRS):
            sides = []
            for k in range(2):
                slot = owner * SLOTS + pair * 2 + k
                r = blocks_ref[0, slot]
                c = blocks_ref[1, slot]
                left = turned_ref[pl.ds(pl.multiple_of(c * SIDE, SIDE), SIDE), :]
                right = hidden_ref[:, pl.ds(pl.multiple_of((r // 2) * LANES, LANES), LANES)]
                product = jnp.dot(left, right, preferred_element_type=jnp.float32)
                sides.append(pltpu.roll(product, ((r + k) % 2) * SIDE, 1))
            out_ref[chip, pl.ds(pair * SIDE, SIDE), :] = jnp.where(low_lane, sides[0], sides[1])
        return carry

    lax.fori_loop(0, out_ref.shape[0], one_chip, 0, unroll=2)


def partner_terms_kernel(core_ref, blocks_ref, hidden_ref, turned_ref, out_ref):
    block_products(1 - core_ref[0], blocks_ref, hidden_ref, turned_ref, out_ref)


def own_terms_kernel(
    core_ref, blocks_ref, hidden_ref, turned_ref, master_in, moment_in, variance_in,
    out_ref, master_ref, moment_ref, variance_ref,
):
    block_products(core_ref[0], blocks_ref, hidden_ref, turned_ref, out_ref)
    master_ref[...] = master_in[...]
    moment_ref[...] = moment_in[...]
    variance_ref[...] = variance_in[...]


def code_kernel(own_ref, other_ref, out_ref):
    def one_chip(chip, carry):
        totals = []
        for pair in range(PAIRS):
            rows = pl.ds(pair * SIDE, SIDE)
            totals.append(own_ref[chip, rows, :] + other_ref[chip, rows, :])
        peak = functools.reduce(jnp.maximum, [jnp.abs(p) for p in totals])
        peak = jnp.max(peak, axis=0, keepdims=True)
        exponent = jnp.floor(jnp.log(jnp.maximum(peak, 1e-30)) * INV_LN2)
        scale = jnp.exp2(CODE_BITS - exponent)
        code = [jnp.round(p * scale).astype(jnp.int32) for p in totals]
        out_ref[chip, pl.ds(0, SIDE), :] = (code[0] << 16) | (code[1] & 0xFFFF)
        out_ref[chip, pl.ds(SIDE, EXP_ROWS), :] = jnp.broadcast_to(
            exponent.astype(jnp.int32), (EXP_ROWS, LANES)
        )
        return carry

    lax.fori_loop(0, out_ref.shape[0], one_chip, 0, unroll=2)


def sum_kernel(me_ref, live_ref, recv_ref, grad_ref, square_ref, turned_ref):
    def add(d, totals):
        high, low = totals
        word = recv_ref[d, pl.ds(0, SIDE), :]
        exponent = recv_ref[d, pl.ds(SIDE, EXP_ROWS), :][:1].astype(jnp.float32)
        scale = jnp.exp2(exponent - CODE_BITS)
        high = high + (word >> 16).astype(jnp.float32) * scale
        low = low + ((word << 16) >> 16).astype(jnp.float32) * scale
        return high, low

    live = live_ref[me_ref[0]]
    zero = jnp.zeros((SIDE, LANES), jnp.float32)
    totals = lax.fori_loop(0, recv_ref.shape[0], add, (zero, zero), unroll=4)
    slot = lax.broadcasted_iota(jnp.int32, (SIDE, LANES), 1) // SIDE
    square = jnp.zeros((SIDE, LANES), jnp.float32)
    for pair in range(PAIRS):
        total = jnp.where(slot + pair * 2 < live, totals[pair], 0.0)
        square = square + total * total
        turned_ref[pair] = jnp.concatenate([total.T, total.T], axis=1)
    low_lane = lax.broadcasted_iota(jnp.int32, (TILES, LANES), 1) < SIDE
    for s in range(SLOTS):
        base = (s % 2) * SIDE
        even = turned_ref[s // 2, pl.ds(base, TILES, stride=2), :]
        odd = turned_ref[s // 2, pl.ds(base + 1, TILES, stride=2), :]
        grad_ref[pl.ds(s, TILES, stride=SLOTS), :] = jnp.where(low_lane, even, odd)
    square_ref[...] = jnp.broadcast_to(jnp.sum(square, keepdims=True), square_ref.shape)


def update_kernel(
    live_ref, square_ref, grad_ref, master_ref, moment_ref, variance_ref,
    new_master_ref, new_moment_ref, new_variance_ref, clipped_ref, own_ref,
):
    live_total = live_ref[0]
    square = square_ref[0, :1]
    for owner in range(1, square_ref.shape[0]):
        live_total = live_total + live_ref[owner]
        square = square + square_ref[owner, :1]
    entries = jnp.full((1, LANES), live_total, jnp.int32).astype(jnp.float32) * BLOCK
    clip = jnp.minimum(1.0, 1.0 / jnp.sqrt(square / entries + 1e-06))
    for t in range(TILES):
        lanes = pl.ds(t * LANES, LANES)
        clipped = clip * grad_ref[pl.ds(t * SLOTS, SLOTS), :]
        moment = 0.9 * moment_ref[:, lanes] + 0.1 * clipped
        variance = 0.95 * variance_ref[:, lanes] + 0.05 * clipped * clipped
        master = master_ref[:, lanes]
        moment_hat = moment / (1.0 - 0.9**20)
        variance_hat = variance / (1.0 - 0.95**20)
        step = moment_hat / (jnp.sqrt(variance_hat) + 1e-08) + 0.1 * master
        master = master - 0.02 * step
        clipped_ref[:, lanes] = clipped
        new_moment_ref[:, lanes] = moment
        new_variance_ref[:, lanes] = variance
        new_master_ref[:, lanes] = master
        own_ref[:, lanes] = master.astype(jnp.bfloat16)


def publish_kernel(core_ref, mine_ref, other_ref, out_ref):
    rows = CORES * SLOTS
    group = 2

    def weave(first_ref, second_ref):
        for chip in range(0, first_ref.shape[0], group):
            parts = []
            for k in range(group):
                parts.append(first_ref[chip + k].astype(jnp.float32))
                parts.append(second_ref[chip + k].astype(jnp.float32))
            block = jnp.concatenate(parts, axis=0).astype(jnp.bfloat16)
            out_ref[pl.ds(chip * rows, group * rows), :] = block

    @pl.when(core_ref[0] == 0)
    def _():
        weave(mine_ref, other_ref)

    @pl.when(core_ref[0] == 1)
    def _():
        weave(other_ref, mine_ref)


VMEM = pl.BlockSpec(memory_space=pltpu.VMEM)
SMEM = pl.BlockSpec(memory_space=pltpu.SMEM)
FLOPS_TURN = 6000
PARAMS = pltpu.CompilerParams(vmem_limit_bytes=40 * 1024 * 1024)


def local(hidden, grad_out, block_list, live_block_count, master, moment, variance):
    chips = lax.axis_size("chip")
    tokens = hidden.shape[0]
    core = lax.axis_index("core").reshape(1)
    me = lax.axis_index(AXES).reshape(1)
    swap = [(0, 1), (1, 0)]
    shape = jax.ShapeDtypeStruct(master.shape, jnp.float32)
    blocks = block_list.T
    cost = pl.CostEstimate(
        flops=2 * chips * SLOTS * SIDE * LANES * tokens,
        bytes_accessed=2 * (hidden.size + grad_out.size),
        transcendentals=0,
    )
    terms = jax.ShapeDtypeStruct((chips, PAIRS * SIDE, LANES), jnp.float32)
    turned = pl.pallas_call(
        turn_kernel,
        out_shape=jax.ShapeDtypeStruct(grad_out.shape[::-1], grad_out.dtype),
        in_specs=[VMEM],
        out_specs=VMEM,
        compiler_params=PARAMS,
        cost_estimate=pl.CostEstimate(
            flops=FLOPS_TURN * grad_out.size, bytes_accessed=4 * grad_out.size, transcendentals=0
        ),
        name="turn_grad_out",
    )(grad_out)
    partner_terms = pl.pallas_call(
        partner_terms_kernel,
        out_shape=terms,
        in_specs=[SMEM, SMEM, VMEM, VMEM],
        out_specs=VMEM,
        compiler_params=PARAMS,
        cost_estimate=cost,
        name="partner_terms",
    )(core, blocks, hidden, turned)
    arrived = lax.ppermute(partner_terms, "core", swap)
    own_terms, master, moment, variance = pl.pallas_call(
        own_terms_kernel,
        out_shape=(terms, shape, shape, shape),
        in_specs=[SMEM, SMEM] + [VMEM] * 5,
        out_specs=(VMEM,) * 4,
        compiler_params=PARAMS,
        cost_estimate=cost,
        name="own_terms",
    )(core, blocks, hidden, turned, master, moment, variance)
    codes = pl.pallas_call(
        code_kernel,
        out_shape=jax.ShapeDtypeStruct((chips, SIDE + EXP_ROWS, LANES), jnp.int32),
        in_specs=[VMEM, VMEM],
        out_specs=VMEM,
        compiler_params=PARAMS,
        name="code_terms",
    )(own_terms, arrived)
    received = lax.all_to_all(codes, "chip", split_axis=0, concat_axis=0, tiled=True)
    gradient, square = pl.pallas_call(
        sum_kernel,
        out_shape=(
            jax.ShapeDtypeStruct((TILES * SLOTS, LANES), jnp.float32),
            jax.ShapeDtypeStruct((chips * CORES, 8, LANES), jnp.float32),
        ),
        in_specs=[SMEM, SMEM, VMEM],
        out_specs=(VMEM, VMEM),
        scratch_shapes=[pltpu.VMEM((PAIRS, LANES, LANES), jnp.float32)],
        compiler_params=PARAMS,
        name="sum_sources",
    )(me, live_block_count, received)
    square = lax.all_to_all(square, AXES[::-1], split_axis=0, concat_axis=0, tiled=True)
    new_master, new_moment, new_variance, clipped, own = pl.pallas_call(
        update_kernel,
        out_shape=(shape, shape, shape, shape, jax.ShapeDtypeStruct(master.shape, jnp.bfloat16)),
        in_specs=[SMEM, VMEM, VMEM, VMEM, VMEM, VMEM],
        out_specs=(VMEM,) * 5,
        compiler_params=PARAMS,
        name="adamw",
    )(live_block_count, square, gradient, master, moment, variance)
    spread = jnp.broadcast_to(own[None], (chips,) + own.shape)
    mine = lax.all_to_all(spread, "chip", split_axis=0, concat_axis=0, tiled=True)
    other = lax.ppermute(mine, "core", swap)
    published = pl.pallas_call(
        publish_kernel,
        out_shape=jax.ShapeDtypeStruct((chips * CORES * SLOTS, BLOCK), jnp.bfloat16),
        in_specs=[SMEM, VMEM, VMEM],
        out_specs=VMEM,
        compiler_params=PARAMS,
        name="publish",
    )(core, mine, other)
    return new_master, new_moment, new_variance, clipped, published


def solution(mesh):
    devices = mesh.devices.reshape(-1, CORES)
    rows = P(AXES, None)
    return jax.shard_map(
        local,
        mesh=Mesh(devices, AXES),
        in_specs=(rows, rows, P(), P(), rows, rows, rows),
        out_specs=(rows, rows, rows, rows, P()),
        check_vma=False,
    )
```

profile of v0, /device:TPU:0, one launch (start us, length us, event | category | flops | bytes accessed | tf_op | source)
XLA Modules:
  0.0 71.4 jit_solution(5987712825610178683)
XLA Ops:
  0.6 0.0 copy-start.6
  0.6 1.3 %copy-done.6 = bf16[256,2560]{1,0:T(8,128)(2,1)S(1)} copy-done((bf16[256,2560]{1,0:T(8,128)(2,1)S(1)}, bf16[256,2560]{1,0:T(8,128)(2,1)}, u32[]{:S(2)}) %copy-start.6) | copy-done | bytes 1310744
  2.0 0.0 copy-start
  2.0 0.0 copy-start.4
  2.0 0.4 turn_grad_out.1.turned_ref
  2.4 1.6 %copy-done = bf16[256,6912]{1,0:T(8,128)(2,1)S(1)} copy-done((bf16[256,6912]{1,0:T(8,128)(2,1)S(1)}, bf16[256,6912]{1,0:T(8,128)(2,1)}, u32[]{:S(2)}) %copy-start) | copy-done | bytes 3538968
  4.0 0.0 copy-done.4
  4.0 0.0 copy-start.1
  4.0 0.0 copy-start.2
  4.0 0.0 copy-start.3
  4.0 3.0 %partner_terms.1 = f32[16,128,128]{2,1,0:T(8,128)S(1)} custom-call(s32[1]{0:T(128)} %bitcast.1.core_ref, s32[2,128]{1,0:T(2,128)S(1)} %bitcast.3, bf16[256,6912]{1,0:T(8,128)(2,1)S(1)} %copy-done, bf16[2560,256]{1,0:T(8,128)(2,1)S(1)} %turn_grad_out.1.turned_ref), custom_call_target="tpu_custom_call" | custom-call | flops 268435456 | bytes 4849664 | tf_op jit(solution)/shard_map/partner_terms/pallas_call | solution.py:193
  7.0 0.5 collective-permute-start
  7.5 0.0 copy-done.1
  7.5 0.0 copy-done.2
  7.5 0.0 copy-done.3
  7.5 3.0 %own_terms.1 = (f32[16,128,128]{2,1,0:T(8,128)S(1)}, f32[4,4096]{1,0:T(4,128)S(1)}, f32[4,4096]{1,0:T(4,128)S(1)}, f32[4,4096]{1,0:T(4,128)S(1)}) custom-call(s32[1]{0:T(128)} %bitcast.1.core_ref, s32[2,128]{1,0:T(2,128)S(1)} %bitcast.4, bf16[256,6912]{1,0:T(8,128)(2,1)S(1)} %copy-done, bf16[2560,256]{1,0:T(8,128)(2,1)S(1)} %turn_grad_out.1.turned_ref, ...), custom_call_target="tpu_custom_call" | custom-call | flops 268435456 | bytes 4849664 | tf_op jit(solution)/shard_map/own_terms/pallas_call | solution.py:203
  10.5 0.0 collective-permute-done.other_ref
  10.5 0.0 copy-start.5
  10.6 1.2 %code_terms.1 = s32[16,72,128]{2,1,0:T(8,128)} custom-call(f32[16,128,128]{2,1,0:T(8,128)S(1)} %get-tuple-element.16.own_ref, f32[16,128,128]{2,1,0:T(8,128)S(1)} %collective-permute-done.other_ref), custom_call_target="tpu_custom_call" | custom-call | tf_op jit(solution)/shard_map/code_terms/pallas_call | solution.py:212
  11.8 7.9 %all-to-all-start = ((s32[16,72,128]{2,1,0:T(8,128)}), s32[16,72,128]{2,1,0:T(8,128)S(1)}, u32[]{:S(2)}, u32[]{:S(2)}) async-start(s32[16,72,128]{2,1,0:T(8,128)} %code_terms.1), calls=%async_computation | async-start | bytes 1179648 | tf_op jit(solution)/shard_map/all_to_all | solution.py:220
  19.7 16.6 %all-to-all-done.recv_ref = s32[16,72,128]{2,1,0:T(8,128)S(1)} async-done(((s32[16,72,128]{2,1,0:T(8,128)}), s32[16,72,128]{2,1,0:T(8,128)S(1)}, u32[]{:S(2)}, u32[]{:S(2)}) %all-to-all-start) | async-done | bytes 589856 | tf_op jit(solution)/shard_map/all_to_all | solution.py:220
  36.3 0.0 copy-done.5
  36.3 0.9 %sum_sources.1 = (f32[128,128]{1,0:T(8,128)S(1)}, f32[32,8,128]{2,1,0:T(8,128)S(1)}) custom-call(s32[1]{0:T(128)} %bitcast.me_ref, s32[32]{0:T(128)S(1)} %copy-done.5, s32[16,72,128]{2,1,0:T(8,128)S(1)} %all-to-all-done.recv_ref), custom_call_target="tpu_custom_call" | custom-call | tf_op jit(solution)/shard_map/sum_sources/pallas_call | solution.py:221
  37.2 11.2 %all_to_all.15.square_ref = f32[32,8,128]{2,1,0:T(8,128)S(1)} all-to-all(f32[32,8,128]{2,1,0:T(8,128)S(1)} %get-tuple-element.17), channel_id=1, replica_groups=mesh['dp'=8,'owner'=4] {'owner':(2)2,'dp','owner':(1)2}, dimensions={0} | all-to-all | bytes 262144 | tf_op jit(solution)/shard_map/all_to_all | solution.py:233
  48.4 1.4 %adamw.1 = (f32[4,4096]{1,0:T(4,128)}, f32[4,4096]{1,0:T(4,128)}, f32[4,4096]{1,0:T(4,128)}, f32[4,4096]{1,0:T(4,128)}, bf16[4,4096]{1,0:T(4,128)(2,1)S(1)}) custom-call(s32[32]{0:T(128)S(1)} %copy-done.5, f32[32,8,128]{2,1,0:T(8,128)S(1)} %all_to_all.15.square_ref, f32[128,128]{1,0:T(8,128)S(1)} %get-tuple-element.18.grad_ref, ...), custom_call_target="tpu_custom_call" | custom-call | tf_op jit(solution)/shard_map/adamw/pallas_call | solution.py:234
  49.8 0.2 broadcast_in_dim.2
  50.0 18.3 %all_to_all.16.mine_ref = bf16[16,4,4096]{2,1,0:T(4,128)(2,1)S(1)} all-to-all(bf16[16,4,4096]{2,1,0:T(4,128)(2,1)S(1)} %broadcast_in_dim.2), channel_id=1, replica_groups=mesh['dp'=8,'owner'=4] {'dp','owner':(1)2}, dimensions={0} | all-to-all | bytes 1048576 | tf_op jit(solution)/shard_map/all_to_all | solution.py:243
  68.3 0.0 collective-permute-start.1
  68.3 1.9 %collective-permute-done.1.other_ref = bf16[16,4,4096]{2,1,0:T(4,128)(2,1)S(1)} collective-permute-done((bf16[16,4,4096]{2,1,0:T(4,128)(2,1)S(1)}, bf16[16,4,4096]{2,1,0:T(4,128)(2,1)S(1)}, u32[]{:S(2)}, u32[]{:S(2)}) %collective-permute-start.1) | collective-permute-done | bytes 524320 | tf_op jit(solution)/shard_map/ppermute | solution.py:244
  70.2 1.2 %publish.1 = bf16[128,4096]{1,0:T(8,128)(2,1)} custom-call(s32[1]{0:T(128)} %bitcast.1.core_ref, bf16[16,4,4096]{2,1,0:T(4,128)(2,1)S(1)} %all_to_all.16.mine_ref, bf16[16,4,4096]{2,1,0:T(4,128)(2,1)S(1)} %collective-permute-done.1.other_ref), custom_call_target="tpu_custom_call" | custom-call | tf_op jit(solution)/shard_map/publish/pallas_call | solution.py:245
Async XLA Ops:
  0.6 1.3 %copy-start.6 = (bf16[256,2560]{1,0:T(8,128)(2,1)S(1)}, bf16[256,2560]{1,0:T(8,128)(2,1)}, u32[]{:S(2)}) copy-start(bf16[256,2560]{1,0:T(8,128)(2,1)} %grad_ref.1) | copy-start | bytes 3932164
  2.0 2.0 %copy-start = (bf16[256,6912]{1,0:T(8,128)(2,1)S(1)}, bf16[256,6912]{1,0:T(8,128)(2,1)}, u32[]{:S(2)}) copy-start(bf16[256,6912]{1,0:T(8,128)(2,1)} %hidden_ref.3) | copy-start | bytes 10616836
  2.0 2.0 %copy-start.4 = (s32[128,2]{0,1:T(2,128)S(1)}, s32[128,2]{0,1:T(2,128)}, u32[]{:S(2)}) copy-start(s32[128,2]{0,1:T(2,128)} %param.9) | copy-start | bytes 3076
  4.0 3.5 %copy-start.1 = (f32[4,4096]{1,0:T(4,128)S(1)}, f32[4,4096]{1,0:T(4,128)}, u32[]{:S(2)}) copy-start(f32[4,4096]{1,0:T(4,128)} %master_in.1) | copy-start | bytes 196612
  4.0 3.5 %copy-start.2 = (f32[4,4096]{1,0:T(4,128)S(1)}, f32[4,4096]{1,0:T(4,128)}, u32[]{:S(2)}) copy-start(f32[4,4096]{1,0:T(4,128)} %moment_in.1) | copy-start | bytes 196612
  4.0 3.5 %copy-start.3 = (f32[4,4096]{1,0:T(4,128)S(1)}, f32[4,4096]{1,0:T(4,128)}, u32[]{:S(2)}) copy-start(f32[4,4096]{1,0:T(4,128)} %variance_in.1) | copy-start | bytes 196612
  7.0 3.6 %collective-permute-start = (f32[16,128,128]{2,1,0:T(8,128)S(1)}, f32[16,128,128]{2,1,0:T(8,128)S(1)}, u32[]{:S(2)}, u32[]{:S(2)}) collective-permute-start(f32[16,128,128]{2,1,0:T(8,128)S(1)} %partner_terms.1), channel_id=1, source_target_pairs={{0,1},{1,0},{2,3},{3,2},{4,5},{5,4},{6,7},{7,6},{8,9},{9,8},{10,11... | collective-permute-start | bytes 3145736 | tf_op jit(solution)/shard_map/ppermute | solution.py:202
  10.5 25.8 %copy-start.5 = (s32[32]{0:T(128)S(1)}, s32[32]{0:T(128)}, u32[]{:S(2)}) copy-start(s32[32]{0:T(128)} %live_ref.3) | copy-start | bytes 388
  11.8 24.5 %all-to-all-start = ((s32[16,72,128]{2,1,0:T(8,128)}), s32[16,72,128]{2,1,0:T(8,128)S(1)}, u32[]{:S(2)}, u32[]{:S(2)}) async-start(s32[16,72,128]{2,1,0:T(8,128)} %code_terms.1), calls=%async_computation | async-start | bytes 1179648 | tf_op jit(solution)/shard_map/all_to_all | solution.py:220
  68.3 1.9 %collective-permute-start.1 = (bf16[16,4,4096]{2,1,0:T(4,128)(2,1)S(1)}, bf16[16,4,4096]{2,1,0:T(4,128)(2,1)S(1)}, u32[]{:S(2)}, u32[]{:S(2)}) collective-permute-start(bf16[16,4,4096]{2,1,0:T(4,128)(2,1)S(1)} %all_to_all.16.mine_ref), channel_id=1, source_target_pairs={{0,1},{1,0},{2,3},{3,2},{4,5},{5,4},{6,7},{7,6},{8,9},{9,8},{10,11... | collective-permute-start | bytes 1572872 | tf_op jit(solution)/shard_map/ppermute | solution.py:244
where the time goes:
time: 71.7 us; the launch traced here: 71.4 us
  blocking collectives  29.5 us (41%)
  waiting for transfers between devices  18.5 us (26%)
  Pallas kernels  11.2 us (16%)
  starting transfers between devices  8.42 us (12%)
  local copies, waits for them, and re-layouts  3.13 us (4%)
  between operations  0.72 us (1%)
    all_to_all x1, blocking collectives, local(): lax.all_to_all(spread, 'chip', split_axis=0, concat_axis=0, tiled=True)  18.3 us
    all_to_all x1, waiting for transfers between devices, local(): lax.all_to_all(codes, 'chip', split_axis=0, concat_axis=0, tiled=True)  16.6 us
    all_to_all x1, blocking collectives, local(): lax.all_to_all(square, AXES[::-1], split_axis=0, concat_axis=0, tiled=True)  11.2 us
    all_to_all x1, starting transfers between devices, local(): lax.all_to_all(codes, 'chip', split_axis=0, concat_axis=0, tiled=True)  7.9 us
    pallas_call x1, Pallas kernels, local(): pl.pallas_call(own_terms_kernel, out_shape=(terms, shape, shape, shape),...  3.02 us
    pallas_call x1, Pallas kernels, local(): pl.pallas_call(partner_terms_kernel, out_shape=terms, in_specs=[SMEM, SME...  3 us
    unnamed x14, local copies, waits for them, and re-layouts  2.94 us
    ppermute x1, waiting for transfers between devices, local(): other = lax.ppermute(mine, 'core', swap)  1.91 us
  transfers between devices with their start and end apart: 3, of which 2 were waited for; matrix products, arithmetic and copies ran while one was open for 0% of the time, Pallas kernels for 4%

commit v1 on v0

v1 whole, which is shorter than its diff:
```python
import functools

import jax
import jax.numpy as jnp
from jax import lax
from jax.experimental import pallas as pl
from jax.experimental.pallas import tpu as pltpu
from jax.sharding import Mesh
from jax.sharding import PartitionSpec as P

SIDE = 64
LANES = 128
SLOTS = 4
PAIRS = SLOTS // 2
BLOCK = SIDE * SIDE
TILES = BLOCK // LANES
EXP_ROWS = 8
CODE_BITS = 13
GRAD_PARTS = 4
HIDDEN_PARTS = 8
STORE_PARTS = 8
CORES = 2
AXES = ("chip", "core")
INV_LN2 = 1.4426950408889634


def block_products(core, blocks_ref, hidden_ref, turned_ref, out_ref):
    low_lane = lax.broadcasted_iota(jnp.int32, (SIDE, LANES), 1) < SIDE

    def one_chip(chip, carry):
        owner = chip * CORES + core
        for pair in range(PAIRS):
            lefts, rights, rows = [], [], []
            for k in range(2):
                slot = owner * SLOTS + pair * 2 + k
                r = blocks_ref[0, slot]
                c = blocks_ref[1, slot]
                lefts.append(turned_ref[pl.ds(pl.multiple_of(c * SIDE, SIDE), SIDE), :])
                lanes = pl.ds(pl.multiple_of((r // 2) * LANES, LANES), LANES)
                rights.append(hidden_ref[:, lanes])
                rows.append(r)
            product = jnp.dot(
                jnp.concatenate(lefts, axis=0),
                jnp.concatenate(rights, axis=1),
                preferred_element_type=jnp.float32,
            )
            first = pltpu.roll(product[:SIDE, :LANES], (rows[0] % 2) * SIDE, 1)
            second = pltpu.roll(product[SIDE:, LANES:], ((rows[1] + 1) % 2) * SIDE, 1)
            out_ref[chip, pl.ds(pair * SIDE, SIDE), :] = jnp.where(low_lane, first, second)
        return carry

    lax.fori_loop(0, out_ref.shape[0], one_chip, 0, unroll=4)


def partner_terms_kernel(
    place_ref, blocks_hbm, hidden_hbm, grad_hbm, master_hbm, moment_hbm, variance_hbm,
    out_ref, hidden_ref, turned_ref, master_ref, moment_ref, variance_ref,
    blocks_ref, grad_ref, sems,
):
    copies = [pltpu.make_async_copy(blocks_hbm, blocks_ref, sems.at[0])]
    for source, target, parts in ((grad_hbm, grad_ref, GRAD_PARTS), (hidden_hbm, hidden_ref, HIDDEN_PARTS)):
        step = source.shape[0] // parts
        for k in range(parts):
            rows = pl.ds(k * step, step)
            copies.append(
                pltpu.make_async_copy(source.at[rows], target.at[rows], sems.at[len(copies)])
            )
    for source, target in (
        (master_hbm, master_ref), (moment_hbm, moment_ref), (variance_hbm, variance_ref)
    ):
        copies.append(pltpu.make_async_copy(source, target, sems.at[len(copies)]))
    for copy in copies:
        copy.start()
    grad_end = 1 + GRAD_PARTS
    hidden_end = grad_end + HIDDEN_PARTS
    for copy in copies[:grad_end]:
        copy.wait()
    for k in range(grad_ref.shape[1] // LANES):
        turned_ref[pl.ds(k * LANES, LANES), :] = grad_ref[:, pl.ds(k * LANES, LANES)].T
    for copy in copies[grad_end:hidden_end]:
        copy.wait()
    block_products(1 - place_ref[0], blocks_ref, hidden_ref, turned_ref, out_ref)
    for copy in copies[hidden_end:]:
        copy.wait()


def own_terms_kernel(
    place_ref, blocks_ref, live_ref, hidden_ref, turned_ref, out_ref, live_rows_ref
):
    block_products(place_ref[0], blocks_ref, hidden_ref, turned_ref, out_ref)
    total = live_ref[0]
    for owner in range(1, live_ref.shape[0]):
        total = total + live_ref[owner]
    live_rows_ref[pl.ds(0, 8), :] = jnp.full((8, LANES), live_ref[place_ref[1]], jnp.int32)
    live_rows_ref[pl.ds(8, 8), :] = jnp.full((8, LANES), total, jnp.int32)


def code_kernel(own_ref, other_ref, out_ref):
    def one_chip(chip, carry):
        totals = []
        for pair in range(PAIRS):
            rows = pl.ds(pair * SIDE, SIDE)
            totals.append(own_ref[chip, rows, :] + other_ref[chip, rows, :])
        peak = functools.reduce(jnp.maximum, [jnp.abs(p) for p in totals])
        peak = jnp.max(peak, axis=0, keepdims=True)
        exponent = jnp.floor(jnp.log(jnp.maximum(peak, 1e-30)) * INV_LN2)
        scale = jnp.exp2(CODE_BITS - exponent)
        code = [jnp.round(p * scale).astype(jnp.int32) for p in totals]
        out_ref[chip, pl.ds(0, SIDE), :] = (code[0] << 16) | (code[1] & 0xFFFF)
        out_ref[chip, pl.ds(SIDE, EXP_ROWS), :] = jnp.broadcast_to(
            exponent.astype(jnp.int32), (EXP_ROWS, LANES)
        )
        return carry

    lax.fori_loop(0, out_ref.shape[0], one_chip, 0, unroll=2)


def sum_kernel(live_ref, recv_ref, grad_ref, square_ref, turned_ref):
    def add(d, totals):
        high, low = totals
        word = recv_ref[d, pl.ds(0, SIDE), :]
        exponent = recv_ref[d, pl.ds(SIDE, EXP_ROWS), :][:1].astype(jnp.float32)
        scale = jnp.exp2(exponent - CODE_BITS)
        high = high + (word >> 16).astype(jnp.float32) * scale
        low = low + ((word << 16) >> 16).astype(jnp.float32) * scale
        return high, low

    live = live_ref[0:1, :]
    zero = jnp.zeros((SIDE, LANES), jnp.float32)
    totals = lax.fori_loop(0, recv_ref.shape[0], add, (zero, zero), unroll=4)
    slot = lax.broadcasted_iota(jnp.int32, (SIDE, LANES), 1) // SIDE
    square = jnp.zeros((SIDE, LANES), jnp.float32)
    for pair in range(PAIRS):
        total = jnp.where(slot + pair * 2 < live, totals[pair], 0.0)
        square = square + total * total
        turned_ref[pair] = jnp.concatenate([total.T, total.T], axis=1)
    low_lane = lax.broadcasted_iota(jnp.int32, (TILES, LANES), 1) < SIDE
    for s in range(SLOTS):
        base = (s % 2) * SIDE
        even = turned_ref[s // 2, pl.ds(base, TILES, stride=2), :]
        odd = turned_ref[s // 2, pl.ds(base + 1, TILES, stride=2), :]
        grad_ref[pl.ds(s, TILES, stride=SLOTS), :] = jnp.where(low_lane, even, odd)
    square = jnp.sum(square, axis=0, keepdims=True)
    square_ref[...] = jnp.broadcast_to(square[None], square_ref.shape)


def update_kernel(
    live_ref, square_ref, grad_ref, master_ref, moment_ref, variance_ref,
    spread_ref, new_master_ref, new_moment_ref, new_variance_ref, clipped_ref,
):
    square = square_ref[0]
    for owner in range(1, square_ref.shape[0]):
        square = square + square_ref[owner]
    square = jnp.sum(square, axis=1, keepdims=True)
    entries = live_ref[8:9, :].astype(jnp.float32) * BLOCK
    clip = jnp.minimum(1.0, 1.0 / jnp.sqrt(square / entries + 1e-06))
    for t in range(TILES):
        lanes = pl.ds(t * LANES, LANES)
        clipped = clip * grad_ref[pl.ds(t * SLOTS, SLOTS), :]
        moment = 0.9 * moment_ref[:, lanes] + 0.1 * clipped
        variance = 0.95 * variance_ref[:, lanes] + 0.05 * clipped * clipped
        master = master_ref[:, lanes]
        moment_hat = moment / (1.0 - 0.9**20)
        variance_hat = variance / (1.0 - 0.95**20)
        step = moment_hat / (jnp.sqrt(variance_hat) + 1e-08) + 0.1 * master
        master = master - 0.02 * step
        clipped_ref[:, lanes] = clipped
        new_moment_ref[:, lanes] = moment
        new_variance_ref[:, lanes] = variance
        new_master_ref[:, lanes] = master
    own = new_master_ref[...].astype(jnp.bfloat16)
    for chip in range(spread_ref.shape[0]):
        spread_ref[chip] = own


def store_kernel(after_ref, *refs):
    half = len(refs) // 2
    for source, target in zip(refs[:half], refs[half:]):
        target[...] = source[...]


def publish_kernel(place_ref, mine_ref, other_ref, out_hbm, woven_ref, sems):
    rows = CORES * SLOTS
    group = sems.shape[0]
    step = mine_ref.shape[0] // group

    def weave(first_ref, second_ref):
        copies = []
        for g in range(group):
            parts = []
            for chip in range(g * step, (g + 1) * step):
                parts.append(first_ref[chip].astype(jnp.float32))
                parts.append(second_ref[chip].astype(jnp.float32))
            block = jnp.concatenate(parts, axis=0).astype(jnp.bfloat16)
            span = pl.ds(g * step * rows, step * rows)
            woven_ref[span, :] = block
            copies.append(
                pltpu.make_async_copy(woven_ref.at[span], out_hbm.at[span], sems.at[g])
            )
            copies[-1].start()
        for copy in copies:
            copy.wait()

    @pl.when(place_ref[0] == 0)
    def _():
        weave(mine_ref, other_ref)

    @pl.when(place_ref[0] == 1)
    def _():
        weave(other_ref, mine_ref)


VMEM = pl.BlockSpec(memory_space=pltpu.VMEM)
SMEM = pl.BlockSpec(memory_space=pltpu.SMEM)
ANY = pl.BlockSpec(memory_space=pl.ANY)
PARAMS = pltpu.CompilerParams(vmem_limit_bytes=40 * 1024 * 1024)


def local(hidden, grad_out, block_list, live_block_count, master, moment, variance):
    chips = lax.axis_size("chip")
    tokens = hidden.shape[0]
    place = jnp.stack([lax.axis_index("core"), lax.axis_index(AXES)])
    swap = [(0, 1), (1, 0)]
    shape = jax.ShapeDtypeStruct(master.shape, jnp.float32)
    kept = pltpu.VMEM(master.shape, jnp.float32)
    blocks = block_list.T
    cost = pl.CostEstimate(
        flops=2 * chips * SLOTS * SIDE * LANES * tokens,
        bytes_accessed=2 * (hidden.size + grad_out.size),
        transcendentals=0,
    )
    terms = pltpu.VMEM((chips, PAIRS * SIDE, LANES), jnp.float32)
    partner_terms, hidden, turned, master, moment, variance = pl.pallas_call(
        partner_terms_kernel,
        out_shape=(
            terms,
            pltpu.VMEM(hidden.shape, hidden.dtype),
            pltpu.VMEM(grad_out.shape[::-1], grad_out.dtype),
            kept,
            kept,
            kept,
        ),
        in_specs=[SMEM] + [ANY] * 6,
        out_specs=(VMEM,) * 6,
        scratch_shapes=[
            pltpu.SMEM(blocks.shape, jnp.int32),
            pltpu.VMEM(grad_out.shape, grad_out.dtype),
            pltpu.SemaphoreType.DMA((4 + GRAD_PARTS + HIDDEN_PARTS,)),
        ],
        compiler_params=PARAMS,
        cost_estimate=cost,
        name="partner_terms",
    )(
        place,
        *(
            pltpu.with_memory_space_constraint(x, pltpu.HBM)
            for x in (blocks, hidden, grad_out, master, moment, variance)
        ),
    )
    arrived = lax.ppermute(partner_terms, "core", swap)
    own_terms, live_rows = pl.pallas_call(
        own_terms_kernel,
        out_shape=(terms, pltpu.VMEM((16, LANES), jnp.int32)),
        in_specs=[SMEM, SMEM, SMEM, VMEM, VMEM],
        out_specs=(VMEM, VMEM),
        compiler_params=PARAMS,
        cost_estimate=cost,
        name="own_terms",
    )(place, blocks, live_block_count, hidden, turned)
    codes = pl.pallas_call(
        code_kernel,
        out_shape=pltpu.VMEM((chips, SIDE + EXP_ROWS, LANES), jnp.int32),
        in_specs=[VMEM, VMEM],
        out_specs=VMEM,
        compiler_params=PARAMS,
        name="code_terms",
    )(own_terms, arrived)
    received = lax.all_to_all(codes, "chip", split_axis=0, concat_axis=0, tiled=True)
    gradient, square = pl.pallas_call(
        sum_kernel,
        out_shape=(
            pltpu.VMEM((TILES * SLOTS, LANES), jnp.float32),
            pltpu.VMEM((chips * CORES, 1, LANES), jnp.float32),
        ),
        in_specs=[VMEM, VMEM],
        out_specs=(VMEM, VMEM),
        scratch_shapes=[pltpu.VMEM((PAIRS, LANES, LANES), jnp.float32)],
        compiler_params=PARAMS,
        name="sum_sources",
    )(live_rows, received)
    square = lax.all_to_all(square, AXES[::-1], split_axis=0, concat_axis=0, tiled=True)
    spread, *updated = pl.pallas_call(
        update_kernel,
        out_shape=(pltpu.VMEM((chips,) + master.shape, jnp.bfloat16), kept, kept, kept, kept),
        in_specs=[VMEM] * 6,
        out_specs=(VMEM,) * 5,
        compiler_params=PARAMS,
        name="adamw",
    )(live_rows, square, gradient, master, moment, variance)
    mine = lax.all_to_all(spread, "chip", split_axis=0, concat_axis=0, tiled=True)
    other = lax.ppermute(mine, "core", swap)
    results = pl.pallas_call(
        store_kernel,
        out_shape=(shape,) * 4,
        in_specs=[ANY] + [VMEM] * 4,
        out_specs=(VMEM,) * 4,
        compiler_params=PARAMS,
        name="store_state",
    )(mine, *updated)
    published = pl.pallas_call(
        publish_kernel,
        out_shape=jax.ShapeDtypeStruct((chips * CORES * SLOTS, BLOCK), jnp.bfloat16),
        in_specs=[SMEM, VMEM, VMEM],
        out_specs=ANY,
        scratch_shapes=[
            pltpu.VMEM((chips * CORES * SLOTS, BLOCK), jnp.bfloat16),
            pltpu.SemaphoreType.DMA((STORE_PARTS,)),
        ],
        compiler_params=PARAMS,
        name="publish",
    )(place, mine, other)
    return (*results, published)


def solution(mesh):
    devices = mesh.devices.reshape(-1, CORES)
    rows = P(AXES, None)
    return jax.shard_map(
        local,
        mesh=Mesh(devices, AXES),
        in_specs=(rows, rows, P(), P(), rows, rows, rows),
        out_specs=(rows, rows, rows, rows, P()),
        check_vma=False,
    )
```

time: 71.7 us -> 65.8 us (0.918)
  blocking collectives: 29.5 us -> 52.7 us
  waiting for transfers between devices: 18.5 us -> 1.21 us
  starting transfers between devices: 8.42 us -> 0.52 us
  local copies, waits for them, and re-layouts: 3.13 us -> 0.01 us
    all_to_all x0 -> x1, blocking collectives: none -> 25.8 us  [local(): lax.all_to_all(codes, 'chip', split_axis=0, concat_axis=0, tiled=True)]
    all_to_all x1 -> x0, waiting for transfers between devices: 16.6 us -> none  [local(): lax.all_to_all(codes, 'chip', split_axis=0, concat_axis=0, tiled=True)]
    all_to_all x1 -> x0, starting transfers between devices: 7.9 us -> none  [local(): lax.all_to_all(codes, 'chip', split_axis=0, concat_axis=0, tiled=True)]
    unnamed x14 -> x4, local copies, waits for them, and re-layouts: 2.94 us -> 0.01 us
    all_to_all x1, blocking collectives: 11.2 us -> 8.89 us  [local(): lax.all_to_all(square, AXES[::-1], split_axis=0, concat_axis=0, tiled=True)]
    pallas_call x6, Pallas kernels: 9.94 us -> 8.86 us  [the longest x1 4.76 us: local(): pl.pallas_call(partner_terms_kernel, out_shape=(terms, pltpu.VMEM(hidden....]
  transfers between devices with their start and end apart: 3 -> 2, of which waited for: 2 -> 1; matrix products, arithmetic and copies ran while one was open for 0% -> 0% of each run, Pallas kernels for 4% -> 5%
where the time goes in v1:
time: 65.8 us; the launch traced here: 65.6 us
  blocking collectives  52.7 us (80%)
  Pallas kernels  10.5 us (16%)
  waiting for transfers between devices  1.21 us (2%)
  between operations  0.7 us (1%)
    all_to_all x1, blocking collectives, local(): lax.all_to_all(codes, 'chip', split_axis=0, concat_axis=0, tiled=True)  25.8 us
    all_to_all x1, blocking collectives, local(): lax.all_to_all(spread, 'chip', split_axis=0, concat_axis=0, tiled=True)  18 us
    all_to_all x1, blocking collectives, local(): lax.all_to_all(square, AXES[::-1], split_axis=0, concat_axis=0, tiled=True)  8.89 us
    pallas_call x1, Pallas kernels, local(): pl.pallas_call(partner_terms_kernel, out_shape=(terms, pltpu.VMEM(hidden....  4.76 us
    pallas_call x1, Pallas kernels, local(): pl.pallas_call(own_terms_kernel, out_shape=(terms, pltpu.VMEM((16, LANES)...  2.32 us
    pallas_call x1, Pallas kernels, local(): pl.pallas_call(publish_kernel, out_shape=jax.ShapeDtypeStruct((chips * CO...  1.6 us
  transfers between devices with their start and end apart: 2, of which 1 were waited for; matrix products, arithmetic and copies ran while one was open for 0% of the time, Pallas kernels for 5%

profile of v1, /device:TPU:0, one launch (start us, length us, event | category | flops | bytes accessed | tf_op | source)
XLA Modules:
  0.0 65.6 jit_solution(15819259657081254633)
XLA Ops:
  0.6 0.0 copy-start
  0.6 0.0 copy-start.1
  0.7 0.1 pad_add_fusion.place_ref
  0.7 4.8 %partner_terms.1 = (f32[16,128,128]{2,1,0:T(8,128)S(1)}, bf16[256,6912]{1,0:T(8,128)(2,1)S(1)}, bf16[2560,256]{1,0:T(8,128)(2,1)S(1)}, f32[4,4096]{1,0:T(4,128)S...) custom-call(s32[2]{0:T(128)S(1)} %pad_add_fusion.place_ref, s32[2,128]{1,0:T(2,128)} %bitcast.3, ...), custom_call_target="tpu_custom_call" | custom-call | flops 268435456 | bytes 4849664 | tf_op jit(solution)/shard_map/partner_terms/pallas_call | solution.py:233
  5.5 0.5 collective-permute-start
  6.0 0.0 copy-done
  6.0 0.0 copy-done.1
  6.0 2.3 %own_terms.1 = (f32[16,128,128]{2,1,0:T(8,128)S(1)}, s32[16,128]{1,0:T(8,128)S(1)}) custom-call(s32[2]{0:T(128)S(1)} %pad_add_fusion.place_ref, s32[2,128]{1,0:T(2,128)S(1)} %bitcast.4, s32[32]{0:T(128)S(1)} %copy-done.1, bf16[256,6912]{1,0:T(8,128)(2,1)S(1)} %get-tuple-element.24.hidden_ref, bf16[2560,256]{1,0:T(8,128)(2,1)S(1)} %get-tuple-element.25.turned_ref), custom_call_target="tpu_custom_call" | custom-call | flops 268435456 | bytes 4849664 | tf_op jit(solution)/shard_map/own_terms/pallas_call | solution.py:261
  8.3 0.0 collective-permute-done.other_ref
  8.4 0.4 code_terms.1
  8.8 25.8 %all_to_all.15.recv_ref = s32[16,72,128]{2,1,0:T(8,128)S(1)} all-to-all(s32[16,72,128]{2,1,0:T(8,128)S(1)} %code_terms.1), channel_id=1, replica_groups=mesh['dp'=8,'owner'=4] {'dp','owner':(1)2}, dimensions={0} | all-to-all | bytes 1179648 | tf_op jit(solution)/shard_map/all_to_all | solution.py:278
  34.6 0.4 sum_sources.1
  35.0 8.9 %all_to_all.16.square_ref = f32[32,1,128]{2,1,0:T(1,128)S(1)} all-to-all(f32[32,1,128]{2,1,0:T(1,128)S(1)} %get-tuple-element.29), channel_id=1, replica_groups=mesh['dp'=8,'owner'=4] {'owner':(2)2,'dp','owner':(1)2}, dimensions={0} | all-to-all | bytes 32768 | tf_op jit(solution)/shard_map/all_to_all | solution.py:291
  43.9 0.3 adamw.1
  44.2 18.0 %all_to_all.17.after_ref.mine_ref = bf16[16,4,4096]{2,1,0:T(4,128)(2,1)S(1)} all-to-all(bf16[16,4,4096]{2,1,0:T(4,128)(2,1)S(1)} %get-tuple-element.34), channel_id=1, replica_groups=mesh['dp'=8,'owner'=4] {'dp','owner':(1)2}, dimensions={0} | all-to-all | bytes 1048576 | tf_op jit(solution)/shard_map/all_to_all | solution.py:300
  62.1 0.0 collective-permute-start.1
  62.1 0.7 %store_state.1 = (f32[4,4096]{1,0:T(4,128)}, f32[4,4096]{1,0:T(4,128)}, f32[4,4096]{1,0:T(4,128)}, f32[4,4096]{1,0:T(4,128)}) custom-call(bf16[16,4,4096]{2,1,0:T(4,128)(2,1)S(1)} %all_to_all.17.after_ref.mine_ref, f32[4,4096]{1,0:T(4,128)S(1)} %get-tuple-element.35.refs_0_, f32[4,4096]{1,0:T(4,128)S(1)} %get-tuple-element.36.refs_1_, ...), custom_call_target="tpu_custom_call" | custom-call | tf_op jit(solution)/shard_map/store_state/pallas_call | solution.py:302
  62.8 1.2 %collective-permute-done.1.other_ref = bf16[16,4,4096]{2,1,0:T(4,128)(2,1)S(1)} collective-permute-done((bf16[16,4,4096]{2,1,0:T(4,128)(2,1)S(1)}, bf16[16,4,4096]{2,1,0:T(4,128)(2,1)S(1)}, u32[]{:S(2)}, u32[]{:S(2)}) %collective-permute-start.1) | collective-permute-done | bytes 524320 | tf_op jit(solution)/shard_map/ppermute | solution.py:301
  64.0 1.6 %publish.1 = bf16[128,4096]{1,0:T(8,128)(2,1)} custom-call(s32[2]{0:T(128)S(1)} %pad_add_fusion.place_ref, bf16[16,4,4096]{2,1,0:T(4,128)(2,1)S(1)} %all_to_all.17.after_ref.mine_ref, bf16[16,4,4096]{2,1,0:T(4,128)(2,1)S(1)} %collective-permute-done.1.other_ref), custom_call_target="tpu_custom_call" | custom-call | tf_op jit(solution)/shard_map/publish/pallas_call | solution.py:310
Async XLA Ops:
  0.6 5.4 %copy-start = (s32[128,2]{0,1:T(2,128)S(1)}, s32[128,2]{0,1:T(2,128)}, u32[]{:S(2)}) copy-start(s32[128,2]{0,1:T(2,128)} %param.9) | copy-start | bytes 3076
  0.6 5.4 %copy-start.1 = (s32[32]{0:T(128)S(1)}, s32[32]{0:T(128)}, u32[]{:S(2)}) copy-start(s32[32]{0:T(128)} %live_ref.1) | copy-start | bytes 388
  5.5 2.8 %collective-permute-start = (f32[16,128,128]{2,1,0:T(8,128)S(1)}, f32[16,128,128]{2,1,0:T(8,128)S(1)}, u32[]{:S(2)}, u32[]{:S(2)}) collective-permute-start(f32[16,128,128]{2,1,0:T(8,128)S(1)} %get-tuple-element.28), channel_id=1, source_target_pairs={{0,1},{1,0},{2,3},{3,2},{4,5},{5,4},{6,7},{7,6},{8,9},{9,8},{10,11... | collective-permute-start | bytes 3145736 | tf_op jit(solution)/shard_map/ppermute | solution.py:260
  62.1 1.9 %collective-permute-start.1 = (bf16[16,4,4096]{2,1,0:T(4,128)(2,1)S(1)}, bf16[16,4,4096]{2,1,0:T(4,128)(2,1)S(1)}, u32[]{:S(2)}, u32[]{:S(2)}) collective-permute-start(bf16[16,4,4096]{2,1,0:T(4,128)(2,1)S(1)} %all_to_all.17.after_ref.mine_ref), channel_id=1, source_target_pairs={{0,1},{1,0},{2,3},{3,2},{4,5},{5,4},{6,7},{7,6},{8,9},{9,8},{10,11... | collective-permute-start | bytes 1572872 | tf_op jit(solution)/shard_map/ppermute | solution.py:301

commit v2 on v1

--- a/solution.py
+++ b/solution.py
@@ -1,4 +1,5 @@
 import functools
+import math
 
 import jax
 import jax.numpy as jnp
@@ -14,11 +15,11 @@
 PAIRS = SLOTS // 2
 BLOCK = SIDE * SIDE
 TILES = BLOCK // LANES
-EXP_ROWS = 8
-CODE_BITS = 13
+LOW_OCTAVE = -36
+LARGEST = 6.0
 GRAD_PARTS = 4
 HIDDEN_PARTS = 8
-STORE_PARTS = 8
+STORE_PARTS = 2
 CORES = 2
 AXES = ("chip", "core")
 INV_LN2 = 1.4426950408889634
@@ -95,35 +96,32 @@
     live_rows_ref[pl.ds(8, 8), :] = jnp.full((8, LANES), total, jnp.int32)
 
 
-def code_kernel(own_ref, other_ref, out_ref):
+def code_kernel(per_octave, own_ref, other_ref, out_ref):
+    def encode(value):
+        octave = jnp.log(jnp.maximum(jnp.abs(value), 2.0**LOW_OCTAVE)) * INV_LN2
+        code = (octave - LOW_OCTAVE) * per_octave
+        return jnp.round(jnp.where(value < 0, -code, code)).astype(jnp.int32)
+
     def one_chip(chip, carry):
-        totals = []
+        code = []
         for pair in range(PAIRS):
             rows = pl.ds(pair * SIDE, SIDE)
-            totals.append(own_ref[chip, rows, :] + other_ref[chip, rows, :])
-        peak = functools.reduce(jnp.maximum, [jnp.abs(p) for p in totals])
-        peak = jnp.max(peak, axis=0, keepdims=True)
-        exponent = jnp.floor(jnp.log(jnp.maximum(peak, 1e-30)) * INV_LN2)
-        scale = jnp.exp2(CODE_BITS - exponent)
-        code = [jnp.round(p * scale).astype(jnp.int32) for p in totals]
-        out_ref[chip, pl.ds(0, SIDE), :] = (code[0] << 16) | (code[1] & 0xFFFF)
-        out_ref[chip, pl.ds(SIDE, EXP_ROWS), :] = jnp.broadcast_to(
-            exponent.astype(jnp.int32), (EXP_ROWS, LANES)
-        )
+            code.append(encode(own_ref[chip, rows, :] + other_ref[chip, rows, :]))
+        out_ref[chip] = (code[0] << 16) | (code[1] & 0xFFFF)
         return carry
 
     lax.fori_loop(0, out_ref.shape[0], one_chip, 0, unroll=2)
 
 
-def sum_kernel(live_ref, recv_ref, grad_ref, square_ref, turned_ref):
+def sum_kernel(per_octave, live_ref, recv_ref, grad_ref, square_ref, turned_ref):
+    def decode(code):
+        value = code.astype(jnp.float32)
+        size = jnp.exp2(jnp.abs(value) * (1.0 / per_octave) + LOW_OCTAVE)
+        return jnp.where(code > 0, size, jnp.where(code < 0, -size, 0.0))
+
     def add(d, totals):
-        high, low = totals
-        word = recv_ref[d, pl.ds(0, SIDE), :]
-        exponent = recv_ref[d, pl.ds(SIDE, EXP_ROWS), :][:1].astype(jnp.float32)
-        scale = jnp.exp2(exponent - CODE_BITS)
-        high = high + (word >> 16).astype(jnp.float32) * scale
-        low = low + ((word << 16) >> 16).astype(jnp.float32) * scale
-        return high, low
+        word = recv_ref[d]
+        return totals[0] + decode(word >> 16), totals[1] + decode((word << 16) >> 16)
 
     live = live_ref[0:1, :]
     zero = jnp.zeros((SIDE, LANES), jnp.float32)
@@ -187,13 +185,14 @@
     def weave(first_ref, second_ref):
         copies = []
         for g in range(group):
-            parts = []
-            for chip in range(g * step, (g + 1) * step):
-                parts.append(first_ref[chip].astype(jnp.float32))
-                parts.append(second_ref[chip].astype(jnp.float32))
-            block = jnp.concatenate(parts, axis=0).astype(jnp.bfloat16)
+            for chip in range(g * step, (g + 1) * step, 2):
+                parts = []
+                for k in range(2):
+                    parts.append(first_ref[chip + k].astype(jnp.float32))
+                    parts.append(second_ref[chip + k].astype(jnp.float32))
+                block = jnp.concatenate(parts, axis=0).astype(jnp.bfloat16)
+                woven_ref[pl.ds(chip * rows, 2 * rows), :] = block
             span = pl.ds(g * step * rows, step * rows)
-            woven_ref[span, :] = block
             copies.append(
                 pltpu.make_async_copy(woven_ref.at[span], out_hbm.at[span], sems.at[g])
             )
@@ -224,6 +223,8 @@
     shape = jax.ShapeDtypeStruct(master.shape, jnp.float32)
     kept = pltpu.VMEM(master.shape, jnp.float32)
     blocks = block_list.T
+    top_octave = math.log2(CORES * tokens * LARGEST * LARGEST) + 0.05
+    per_octave = 32767 / (top_octave - LOW_OCTAVE)
     cost = pl.CostEstimate(
         flops=2 * chips * SLOTS * SIDE * LANES * tokens,
         bytes_accessed=2 * (hidden.size + grad_out.size),
@@ -268,8 +269,8 @@
         name="own_terms",
     )(place, blocks, live_block_count, hidden, turned)
     codes = pl.pallas_call(
-        code_kernel,
-        out_shape=pltpu.VMEM((chips, SIDE + EXP_ROWS, LANES), jnp.int32),
+        functools.partial(code_kernel, per_octave),
+        out_shape=pltpu.VMEM((chips, SIDE, LANES), jnp.int32),
         in_specs=[VMEM, VMEM],
         out_specs=VMEM,
         compiler_params=PARAMS,
@@ -277,7 +278,7 @@
     )(own_terms, arrived)
     received = lax.all_to_all(codes, "chip", split_axis=0, concat_axis=0, tiled=True)
     gradient, square = pl.pallas_call(
-        sum_kernel,
+        functools.partial(sum_kernel, per_octave),
         out_shape=(
             pltpu.VMEM((TILES * SLOTS, LANES), jnp.float32),
             pltpu.VMEM((chips * CORES, 1, LANES), jnp.float32),

time: 65.8 us -> 64.9 us (0.986)
  blocking collectives: 52.7 us -> 51.3 us
    all_to_all x1, blocking collectives: 25.8 us -> 23.4 us  [local(): lax.all_to_all(codes, 'chip', split_axis=0, concat_axis=0, tiled=True)]
    all_to_all x1, blocking collectives: 8.89 us -> 9.86 us  [local(): lax.all_to_all(square, AXES[::-1], split_axis=0, concat_axis=0, tiled=True)]
where the time goes in v2:
time: 64.9 us; the launch traced here: 64.7 us
  blocking collectives  51.3 us (79%)
  Pallas kernels  10.9 us (17%)
  waiting for transfers between devices  1.21 us (2%)
  between operations  0.7 us (1%)
    all_to_all x1, blocking collectives, local(): lax.all_to_all(codes, 'chip', split_axis=0, concat_axis=0, tiled=True)  23.4 us
    all_to_all x1, blocking collectives, local(): lax.all_to_all(spread, 'chip', split_axis=0, concat_axis=0, tiled=True)  18 us
    all_to_all x1, blocking collectives, local(): lax.all_to_all(square, AXES[::-1], split_axis=0, concat_axis=0, tiled=True)  9.86 us
    pallas_call x1, Pallas kernels, local(): pl.pallas_call(partner_terms_kernel, out_shape=(terms, pltpu.VMEM(hidden....  4.75 us
    pallas_call x1, Pallas kernels, local(): pl.pallas_call(own_terms_kernel, out_shape=(terms, pltpu.VMEM((16, LANES)...  2.32 us
    pallas_call x1, Pallas kernels, local(): pl.pallas_call(publish_kernel, out_shape=jax.ShapeDtypeStruct((chips * CO...  1.65 us
  transfers between devices with their start and end apart: 2, of which 1 were waited for; matrix products, arithmetic and copies ran while one was open for 0% of the time, Pallas kernels for 5%

profile of v2, /device:TPU:0, one launch (start us, length us, event | category | flops | bytes accessed | tf_op | source)
XLA Modules:
  0.0 64.7 jit_solution(16685321365561416045)
XLA Ops:
  0.6 0.0 copy-start
  0.6 0.0 copy-start.1
  0.7 0.1 pad_add_fusion.place_ref
  0.7 4.7 %partner_terms.1 = (f32[16,128,128]{2,1,0:T(8,128)S(1)}, bf16[256,6912]{1,0:T(8,128)(2,1)S(1)}, bf16[2560,256]{1,0:T(8,128)(2,1)S(1)}, f32[4,4096]{1,0:T(4,128)S...) custom-call(s32[2]{0:T(128)S(1)} %pad_add_fusion.place_ref, s32[2,128]{1,0:T(2,128)} %bitcast.3, ...), custom_call_target="tpu_custom_call" | custom-call | flops 268435456 | bytes 4849664 | tf_op jit(solution)/shard_map/partner_terms/pallas_call | solution.py:234
  5.5 0.5 collective-permute-start
  6.0 0.0 copy-done
  6.0 0.0 copy-done.1
  6.0 2.3 %own_terms.1 = (f32[16,128,128]{2,1,0:T(8,128)S(1)}, s32[16,128]{1,0:T(8,128)S(1)}) custom-call(s32[2]{0:T(128)S(1)} %pad_add_fusion.place_ref, s32[2,128]{1,0:T(2,128)S(1)} %bitcast.4, s32[32]{0:T(128)S(1)} %copy-done.1, bf16[256,6912]{1,0:T(8,128)(2,1)S(1)} %get-tuple-element.24.hidden_ref, bf16[2560,256]{1,0:T(8,128)(2,1)S(1)} %get-tuple-element.25.turned_ref), custom_call_target="tpu_custom_call" | custom-call | flops 268435456 | bytes 4849664 | tf_op jit(solution)/shard_map/own_terms/pallas_call | solution.py:262
  8.3 0.0 collective-permute-done.other_ref
  8.3 0.6 code_terms.1
  8.9 23.4 %all_to_all.15.recv_ref = s32[16,64,128]{2,1,0:T(8,128)S(1)} all-to-all(s32[16,64,128]{2,1,0:T(8,128)S(1)} %code_terms.1), channel_id=1, replica_groups=mesh['dp'=8,'owner'=4] {'dp','owner':(1)2}, dimensions={0} | all-to-all | bytes 1048576 | tf_op jit(solution)/shard_map/all_to_all | solution.py:279
  32.3 0.6 sum_sources.1
  33.0 9.9 %all_to_all.16.square_ref = f32[32,1,128]{2,1,0:T(1,128)S(1)} all-to-all(f32[32,1,128]{2,1,0:T(1,128)S(1)} %get-tuple-element.29), channel_id=1, replica_groups=mesh['dp'=8,'owner'=4] {'owner':(2)2,'dp','owner':(1)2}, dimensions={0} | all-to-all | bytes 32768 | tf_op jit(solution)/shard_map/all_to_all | solution.py:292
  42.9 0.3 adamw.1
  43.2 18.0 %all_to_all.17.after_ref.mine_ref = bf16[16,4,4096]{2,1,0:T(4,128)(2,1)S(1)} all-to-all(bf16[16,4,4096]{2,1,0:T(4,128)(2,1)S(1)} %get-tuple-element.34), channel_id=1, replica_groups=mesh['dp'=8,'owner'=4] {'dp','owner':(1)2}, dimensions={0} | all-to-all | bytes 1048576 | tf_op jit(solution)/shard_map/all_to_all | solution.py:301
  61.1 0.0 collective-permute-start.1
  61.1 0.7 %store_state.1 = (f32[4,4096]{1,0:T(4,128)}, f32[4,4096]{1,0:T(4,128)}, f32[4,4096]{1,0:T(4,128)}, f32[4,4096]{1,0:T(4,128)}) custom-call(bf16[16,4,4096]{2,1,0:T(4,128)(2,1)S(1)} %all_to_all.17.after_ref.mine_ref, f32[4,4096]{1,0:T(4,128)S(1)} %get-tuple-element.35.refs_0_, f32[4,4096]{1,0:T(4,128)S(1)} %get-tuple-element.36.refs_1_, ...), custom_call_target="tpu_custom_call" | custom-call | tf_op jit(solution)/shard_map/store_state/pallas_call | solution.py:303
  61.8 1.2 %collective-permute-done.1.other_ref = bf16[16,4,4096]{2,1,0:T(4,128)(2,1)S(1)} collective-permute-done((bf16[16,4,4096]{2,1,0:T(4,128)(2,1)S(1)}, bf16[16,4,4096]{2,1,0:T(4,128)(2,1)S(1)}, u32[]{:S(2)}, u32[]{:S(2)}) %collective-permute-start.1) | collective-permute-done | bytes 524320 | tf_op jit(solution)/shard_map/ppermute | solution.py:302
  63.0 1.6 %publish.1 = bf16[128,4096]{1,0:T(8,128)(2,1)} custom-call(s32[2]{0:T(128)S(1)} %pad_add_fusion.place_ref, bf16[16,4,4096]{2,1,0:T(4,128)(2,1)S(1)} %all_to_all.17.after_ref.mine_ref, bf16[16,4,4096]{2,1,0:T(4,128)(2,1)S(1)} %collective-permute-done.1.other_ref), custom_call_target="tpu_custom_call" | custom-call | tf_op jit(solution)/shard_map/publish/pallas_call | solution.py:311
Async XLA Ops:
  0.6 5.4 %copy-start = (s32[128,2]{0,1:T(2,128)S(1)}, s32[128,2]{0,1:T(2,128)}, u32[]{:S(2)}) copy-start(s32[128,2]{0,1:T(2,128)} %param.9) | copy-start | bytes 3076
  0.6 5.4 %copy-start.1 = (s32[32]{0:T(128)S(1)}, s32[32]{0:T(128)}, u32[]{:S(2)}) copy-start(s32[32]{0:T(128)} %live_ref.1) | copy-start | bytes 388
  5.5 2.8 %collective-permute-start = (f32[16,128,128]{2,1,0:T(8,128)S(1)}, f32[16,128,128]{2,1,0:T(8,128)S(1)}, u32[]{:S(2)}, u32[]{:S(2)}) collective-permute-start(f32[16,128,128]{2,1,0:T(8,128)S(1)} %get-tuple-element.28), channel_id=1, source_target_pairs={{0,1},{1,0},{2,3},{3,2},{4,5},{5,4},{6,7},{7,6},{8,9},{9,8},{10,11... | collective-permute-start | bytes 3145736 | tf_op jit(solution)/shard_map/ppermute | solution.py:261
  61.1 1.9 %collective-permute-start.1 = (bf16[16,4,4096]{2,1,0:T(4,128)(2,1)S(1)}, bf16[16,4,4096]{2,1,0:T(4,128)(2,1)S(1)}, u32[]{:S(2)}, u32[]{:S(2)}) collective-permute-start(bf16[16,4,4096]{2,1,0:T(4,128)(2,1)S(1)} %all_to_all.17.after_ref.mine_ref), channel_id=1, source_target_pairs={{0,1},{1,0},{2,3},{3,2},{4,5},{5,4},{6,7},{7,6},{8,9},{9,8},{10,11... | collective-permute-start | bytes 1572872 | tf_op jit(solution)/shard_map/ppermute | solution.py:302
